TPU v7x, 128 devices: a whole 4x4x4 slice. The times are simulated.
128 devices in a mesh: lat: 16 (over y, x), lev: 8 (over z, core).
Axes of the slice: x: 4, y: 4, z: 4, core: 2. Of those that a mesh axis runs over, the one named last changes fastest.
Arguments:
- fourier: bfloat16 [32, 2, 2560, 1280], P('lev', None, 'lat'), may hold values from -6 to 6
- loop_len: int32 [1280], replicated, may hold values from 20 to 5148, as said below
- pair_m: int32 [640], replicated, may hold values from 0 to 639, each once
- legendre: bfloat16 [640, 1281, 1280], P(('lat', 'lev')), may hold values from -0.15625 to 0.15625
Outputs:
- spectrum: float32 [640, 1281, 64], P(('lat', 'lev'))
Inputs may be any that keep to these rules, and one draw needn't show every extreme that they name: `loop_len`: loop lengths of one hemisphere from the pole to the equator, each a multiple of 4; the loop next to the pole has the fewest points, the one next to the equator the most. Slot s holds the wavenumbers pair_m[s] and 1279 - pair_m[s]; every value appears once.
All inputs are finite; a program needn't handle non-finite values.
Results may differ from a plain program's by a relative error of at most 0.0031.
Values may be sent and summed in bfloat16 or wider, within the bound.
No kernel may reach another device: no remote copies, remote signals or barrier semaphores. Data moves between devices by JAX's collectives and lax.ppermute only.
A program may use at most 128 MiB of HBM per device.

v0:
```python
import jax
import jax.numpy as jnp
from jax import lax
from jax.sharding import PartitionSpec as P


def swapped(value, axis, apart):
    mask = 2**apart
    pairs = [(source, source ^ mask) for source in range(lax.axis_size(axis))]
    return lax.ppermute(value, axis, pairs)


def shards(fourier, loop_len, pair_m, legendre):
    level_count, _, loop_count, wave_count = fourier.shape
    pairs_here, slot_count, pole_count = legendre.shape
    lat_size = lax.axis_size("lat")
    levels_per_device = lax.axis_size("lev")
    band_count = lat_size // 2
    latitude_position = lax.axis_index("lat")
    lev_place = lax.axis_index("lev")
    hemisphere = latitude_position // band_count
    band_place = latitude_position % band_count
    lengths = lax.dynamic_slice_in_dim(loop_len, band_place * loop_count, loop_count)
    limits = jnp.minimum(wave_count, lengths // 2)
    inside = jnp.arange(wave_count, dtype=jnp.int32)[None, :] < limits[:, None]
    masked = jnp.where(inside, fourier, jnp.zeros((), jnp.bfloat16))
    device_count = lat_size * levels_per_device
    lower_all = pair_m.reshape(device_count, pairs_here)
    columns = jnp.stack([lower_all, wave_count - 1 - lower_all], -1).reshape(-1)
    selector = (columns[:, None] == jnp.arange(wave_count, dtype=jnp.int32)[None, :]).astype(
        jnp.bfloat16
    )
    half_levels = level_count // 2
    local_portion = lax.dynamic_slice_in_dim(masked, hemisphere * half_levels, half_levels, 0)
    give_part = lax.dynamic_slice_in_dim(masked, (1 - hemisphere) * half_levels, half_levels, 0)
    mirrored = swapped(give_part, "lat", lat_size.bit_length() - 2)
    own_float = local_portion.astype(jnp.float32)
    mirror_float = mirrored.astype(jnp.float32)
    flip_sign = (1 - 2 * hemisphere).astype(jnp.float32)
    symmetric = (own_float + mirror_float).astype(jnp.bfloat16)
    antisymmetric = ((own_float - mirror_float) * flip_sign).astype(jnp.bfloat16)
    stacked = jnp.stack([symmetric, antisymmetric], 0)
    group_count = 2
    picked = jnp.einsum(
        "qm,gdcrm->qgdcr", selector, stacked, preferred_element_type=jnp.float32
    ).astype(jnp.bfloat16)
    outgoing = picked.reshape(
        device_count, pairs_here, 2, group_count, half_levels, 2, 1, loop_count
    )
    arrived = lax.all_to_all(outgoing, ("lat", "lev"), split_axis=0, concat_axis=6, tiled=True)
    arrived = arrived.reshape(
        pairs_here, 2, group_count, half_levels, 2, 2, band_count, levels_per_device, loop_count
    )
    sym_data = arrived[:, :, 0]
    anti_data = arrived[:, :, 1]
    einsum_form = "pkbr,pwjchblr->pkwclhj"
    table = legendre.reshape(pairs_here, slot_count, band_count, loop_count)
    sym_rows = wave_count // 2 + 1
    anti_rows = slot_count - sym_rows
    sym_out = jnp.einsum(
        einsum_form, table[:, :sym_rows], sym_data, preferred_element_type=jnp.float32
    )
    anti_out = jnp.einsum(
        einsum_form, table[:, sym_rows:], anti_data, preferred_element_type=jnp.float32
    )
    sym_out = sym_out.reshape(pairs_here, sym_rows, 2, -1)
    anti_out = anti_out.reshape(pairs_here, anti_rows, 2, -1)
    owner_place = latitude_position * levels_per_device + lev_place
    lower_here = lax.dynamic_slice_in_dim(pair_m, owner_place * pairs_here, pairs_here)
    sym_limit = (wave_count - lower_here + 1) // 2
    anti_limit = (wave_count - lower_here) // 2
    sym_index = jnp.arange(sym_rows, dtype=jnp.int32)
    anti_index = jnp.arange(anti_rows, dtype=jnp.int32)
    sym_pick = jnp.where(
        sym_index[None, :, None] < sym_limit[:, None, None], sym_out[:, :, 0], sym_out[:, :, 1]
    )
    anti_pick = jnp.where(
        anti_index[None, :, None] < anti_limit[:, None, None], anti_out[:, :, 0], anti_out[:, :, 1]
    )
    return jnp.concatenate([sym_pick, anti_pick], 1)


def solution(mesh):
    return jax.shard_map(
        shards,
        mesh=mesh,
        in_specs=(P("lev", None, "lat", None), P(), P(), P(("lat", "lev"), None, None)),
        out_specs=P(("lat", "lev"), None, None),
        check_vma=False,
    )
```

profile of v0, /device:TPU:1, one launch (start us, length us, event | category | flops | bytes accessed | tf_op | source)
XLA Modules:
  0.0 164.2 jit_solution(10131862664156205713)
XLA Ops:
  0.0 0.8 fusion.21
  0.8 0.2 iota_compare_fusion.1
  1.0 2.5 %broadcast_select_fusion = bf16[4,2,160,1280]{3,2,1,0:T(8,128)(2,1)S(1)} fusion(bf16[4,2,160,1280]{3,2,1,0:T(8,128)(2,1)} %param.4, pred[160,1280]{1,0:T(8,128)(4,1)S(1)} %iota_compare_fusion.1), kind=kLoop, calls=%fused_computation.17 | loop fusion | flops 1638400 | bytes 6758400 | tf_op jit(solution)/shard_map/jit(_where)/select_n | solution.py:26
  3.5 0.0 copy-start.2
  3.5 1.3 constant_dynamic-slice_fusion
  4.8 3.7 %collective-permute-start = (bf16[2,2,160,1280]{3,2,1,0:T(8,128)(2,1)}, bf16[2,2,160,1280]{3,2,1,0:T(8,128)(2,1)}, u32[]{:S(2)}, u32[]{:S(2)}) collective-permute-start(bf16[2,2,160,1280]{3,2,1,0:T(8,128)(2,1)} %constant_dynamic-slice_fusion), channel_id=1, source_target_pairs={{0,64},{8,72},{16,80},{24,88},{32,96},{40,104},{48,112},{56,120},{... | collective-permute-start | bytes 4915208 | tf_op jit(solution)/shard_map/ppermute | solution.py:10
  8.5 0.0 copy-done.2
  8.5 0.2 stack_reshape.3
  8.8 1.7 %copy.28 = s32[128,5,2]{2,1,0:T(8,128)} copy(s32[128,5,2]{1,0,2:T(8,128)S(1)} %pad_add_fusion) | data formatting | bytes 10240 | tf_op jit(solution)/shard_map/stack | solution.py:29
  10.4 1.2 eq.17
  11.7 32.4 %collective-permute-done = bf16[2,2,160,1280]{3,2,1,0:T(8,128)(2,1)} collective-permute-done((bf16[2,2,160,1280]{3,2,1,0:T(8,128)(2,1)}, bf16[2,2,160,1280]{3,2,1,0:T(8,128)(2,1)}, u32[]{:S(2)}, u32[]{:S(2)}) %collective-permute-start) | collective-permute-done | bytes 1638432 | tf_op jit(solution)/shard_map/ppermute | solution.py:10
  44.1 2.2 %fusion.16 = (bf16[1,2,2,160,1280]{4,3,2,1,0:T(8,128)(2,1)S(1)}, bf16[1,2,2,160,1280]{4,3,2,1,0:T(8,128)(2,1)S(1)}) fusion(bf16[2,2,160,1280]{3,2,1,0:T(8,128)(2,1)} %collective-permute-done, bf16[4,2,160,1280]{3,2,1,0:T(8,128)(2,1)S(1)} %broadcast_select_fusion, s32[]{:T(128)S(6)} %select_n.55, f32[]{:T(128)S(6)} %convert_element_type.22), kind=kLoop, calls=%fused_computation.22 | loop fusion | flops 5734400 | bytes 6553608 | tf_op jit(solution)/shard_map/stack | solution.py:42
  46.3 5.0 %fusion.5 = bf16[1280,2,2,2,160]{0,4,3,2,1:T(8,128)(2,1)S(1)} fusion(bf16[1,2,2,160,1280]{4,3,2,1,0:T(8,128)(2,1)S(1)} %get-tuple-element.6, bf16[1,2,2,160,1280]{4,3,2,1,0:T(8,128)(2,1)S(1)} %get-tuple-element.5, s32[1280]{0:T(1024)S(1)} %eq.17), kind=kOutput, calls=%fused_computation.7 | convolution fusion | flops 4204134400 | bytes 6558720 | tf_op jit(solution)/shard_map/qm,gdcrm->qgdcr/dot_general | solution.py:44
  51.4 9.6 %copy.29 = bf16[1280,2,2,2,160]{4,3,2,1,0:T(2,128)(2,1)} copy(bf16[1280,2,2,2,160]{0,4,3,2,1:T(8,128)(2,1)S(1)} %fusion.5) | data formatting | bytes 6553600 | tf_op jit(solution)/shard_map/convert_element_type | solution.py:46
  61.0 12.0 %all-to-all-start = ((bf16[128,5,2,2,2,2,1,160]{7,5,4,3,2,1,6,0:T(2,128)(2,1)}), bf16[128,5,2,2,2,2,1,160]{7,5,4,3,2,1,6,0:T(2,128)(2,1)}, u32[]{:S(2)}, u32[]{:S(2)}) async-start(bf16[128,5,2,2,2,2,1,160]{7,5,4,3,2,1,6,0:T(2,128)(2,1)} %bitcast.69), calls=%async_computation | async-start | bytes 10485760 | tf_op jit(solution)/shard_map/all_to_all | solution.py:50
  73.0 22.6 %copy.32 = bf16[5,1281,1280]{1,2,0:T(8,128)(2,1)} copy(bf16[5,1281,1280]{2,1,0:T(8,128)(2,1)} %param.7) | data formatting | bytes 32793600 | tf_op args[3]
  95.6 0.1 and_select_fusion.2
  95.7 0.1 iota_compare_fusion.3
  95.8 0.1 iota_compare_fusion.2
  95.8 42.4 %all-to-all-done = bf16[128,5,2,2,2,2,1,160]{7,5,4,3,2,1,6,0:T(2,128)(2,1)} async-done(((bf16[128,5,2,2,2,2,1,160]{7,5,4,3,2,1,6,0:T(2,128)(2,1)}), bf16[128,5,2,2,2,2,1,160]{7,5,4,3,2,1,6,0:T(2,128)(2,1)}, u32[]{:S(2)}, u32[]{:S(2)}) %all-to-all-start) | async-done | bytes 3276832 | tf_op jit(solution)/shard_map/all_to_all | solution.py:50
  138.3 0.0 copy-start
  138.3 4.6 %copy.31 = bf16[1,5,2,2,2,2,128,1,160]{8,6,5,4,2,1,3,7,0:T(8,128)(2,1)S(1)} copy(bf16[1,5,2,2,2,2,128,1,160]{8,5,4,3,2,1,6,7,0:T(2,128)(2,1)} %bitcast.7) | data formatting | bytes 6553600 | tf_op jit(solution)/shard_map/all_to_all | solution.py:50
  142.8 9.2 %fusion.18 = f32[5,640,2,2,8,2,2]{1,4,5,3,6,2,0:T(8,128)} fusion(bf16[5,1281,8,160]{1,3,2,0:T(8,128)(2,1)} %bitcast.70, bf16[5,2,2,2,2,2,8,8,160]{8,7,6,5,4,3,1,0,2:T(8,128)(2,1)S(1)} %bitcast.74), kind=kOutput, calls=%fused_computation.24 | convolution fusion | flops 1048576000 | bytes 12451840 | tf_op jit(solution)/shard_map/pkbr,pwjchblr->pkwclhj/dot_general | solution.py:63
  152.1 0.0 copy-done
  152.1 3.0 %fusion.17 = f32[5,641,2,2,8,2,2]{1,4,5,3,6,2,0:T(8,128)} fusion(bf16[5,1281,8,160]{1,3,2,0:T(8,128)(2,1)S(1)} %bitcast.71, bf16[5,2,2,2,2,2,8,8,160]{8,7,6,5,4,3,1,0,2:T(8,128)(2,1)S(1)} %bitcast.75), kind=kOutput, calls=%fused_computation.23 | convolution fusion | flops 1050214400 | bytes 14092800 | tf_op jit(solution)/shard_map/pkbr,pwjchblr->pkwclhj/dot_general | solution.py:60
  155.1 0.0 copy-start.1
  155.1 3.2 %copy.33 = f32[5,641,2,2,8,2,2]{1,2,6,5,4,3,0:T(2,128)S(1)} copy(f32[5,641,2,2,8,2,2]{1,4,5,3,6,2,0:T(8,128)} %fusion.17) | data formatting | bytes 3281920 | tf_op jit(solution)/shard_map/pkbr,pwjchblr->pkwclhj/transpose | solution.py:60
  158.3 0.0 copy-done.1
  158.3 1.3 copy.35
  159.6 1.3 fusion.24
  160.9 1.5 fusion.23
  162.4 0.1 fusion.20
  162.5 0.1 fusion.19
  162.6 1.6 pad_maximum_fusion
  (2 shorter events, 0.0 us)
Async XLA Ops:
  3.5 5.0 %copy-start.2 = (s32[640]{0:T(1024)S(1)}, s32[640]{0:T(1024)}, u32[]{:S(2)}) copy-start(s32[640]{0:T(1024)} %param.6) | copy-start | bytes 7684
  4.8 39.3 %collective-permute-start = (bf16[2,2,160,1280]{3,2,1,0:T(8,128)(2,1)}, bf16[2,2,160,1280]{3,2,1,0:T(8,128)(2,1)}, u32[]{:S(2)}, u32[]{:S(2)}) collective-permute-start(bf16[2,2,160,1280]{3,2,1,0:T(8,128)(2,1)} %constant_dynamic-slice_fusion), channel_id=1, source_target_pairs={{0,64},{8,72},{16,80},{24,88},{32,96},{40,104},{48,112},{56,120},{... | collective-permute-start | bytes 4915208 | tf_op jit(solution)/shard_map/ppermute | solution.py:10
  61.0 77.3 %all-to-all-start = ((bf16[128,5,2,2,2,2,1,160]{7,5,4,3,2,1,6,0:T(2,128)(2,1)}), bf16[128,5,2,2,2,2,1,160]{7,5,4,3,2,1,6,0:T(2,128)(2,1)}, u32[]{:S(2)}, u32[]{:S(2)}) async-start(bf16[128,5,2,2,2,2,1,160]{7,5,4,3,2,1,6,0:T(2,128)(2,1)} %bitcast.69), calls=%async_computation | async-start | bytes 10485760 | tf_op jit(solution)/shard_map/all_to_all | solution.py:50
  138.3 13.8 %copy-start = (bf16[5,1281,1280]{1,2,0:T(8,128)(2,1)S(1)}, bf16[5,1281,1280]{1,2,0:T(8,128)(2,1)}, u32[]{:S(2)}) copy-start(bf16[5,1281,1280]{1,2,0:T(8,128)(2,1)} %copy.32) | copy-start | bytes 49190404
  155.1 3.2 %copy-start.1 = (f32[5,640,2,2,8,2,2]{1,4,5,3,6,2,0:T(8,128)S(1)}, f32[5,640,2,2,8,2,2]{1,4,5,3,6,2,0:T(8,128)}, u32[]{:S(2)}) copy-start(f32[5,640,2,2,8,2,2]{1,4,5,3,6,2,0:T(8,128)} %fusion.18) | copy-start | bytes 4915204
where the time goes:
time: 165 us; the launch traced here: 164 us
  waiting for transfers between devices  74.8 us (45%)
  local copies, waits for them, and re-layouts  48.4 us (29%)
  matrix products  17.3 us (10%)
  starting transfers between devices  15.7 us (10%)
  other arithmetic  7.78 us (5%)
    all_to_all x1, waiting for transfers between devices, shards(): lax.all_to_all(outgoing, ('lat', 'lev'), split_axis=0, concat_axis=6, til...  42.4 us
    ppermute x1, waiting for transfers between devices, swapped(): return lax.ppermute(value, axis, pairs)  32.4 us
    unnamed x7, local copies, waits for them, and re-layouts  22.6 us
    all_to_all x1, starting transfers between devices, shards(): lax.all_to_all(outgoing, ('lat', 'lev'), split_axis=0, concat_axis=6, til...  12 us
    convert_element_type x1, local copies, waits for them, and re-layouts, shards(): picked = jnp.einsum('qm,gdcrm->qgdcr', selector, stacked, preferred_eleme...  9.62 us
    dot_general x1, matrix products, shards(): jnp.einsum(einsum_form, table[:, sym_rows:], anti_data, preferred_element...  9.22 us
    dot_general x1, matrix products, shards(): jnp.einsum('qm,gdcrm->qgdcr', selector, stacked, preferred_element_type=j...  5.03 us
    all_to_all x1, local copies, waits for them, and re-layouts, shards(): lax.all_to_all(outgoing, ('lat', 'lev'), split_axis=0, concat_axis=6, til...  4.55 us
  transfers between devices with their start and end apart: 2, of which 2 were waited for; matrix products, arithmetic and copies ran while one was open for 16% of the time, Pallas kernels for 0%

commit v1 on v0

v1 whole, which is shorter than its diff:
```python
import functools

import jax
import jax.numpy as jnp
from jax import lax
from jax.experimental import pallas as pl
from jax.experimental.pallas import tpu as pltpu
from jax.sharding import PartitionSpec as P

LANES = 128
SLAB = 32
CHUNK = 104
NT = (((1,), (1,)), ((), ()))


def pick_kernel(pair_ref, len_ref, four_ref, out_ref, table, main, tail, wide):
    parts, band, waves = four_ref.shape
    half = waves // 2
    owners, slots = pair_ref.shape
    bands = len_ref.shape[0]
    place = lax.rem(lax.axis_index("lat"), bands)
    turn = lax.rem(place, 4)

    lane = lax.broadcasted_iota(jnp.int32, (owners, half), 1)
    for s in range(slots):
        low = pair_ref[:, s : s + 1]
        rows = pl.ds(s * owners, owners)
        table[0, rows, :] = jnp.where(lane == low, 1.0, 0.0).astype(jnp.bfloat16)
        table[1, rows, :] = jnp.where(lane == half - 1 - low, 1.0, 0.0).astype(jnp.bfloat16)

    limit = jnp.minimum(waves, lax.shift_right_logical(len_ref[pl.ds(place, 1), :], 1))
    column = jnp.transpose(jnp.broadcast_to(limit, (LANES, limit.shape[1])))
    lane = lax.broadcasted_iota(jnp.int32, (SLAB, LANES), 1)
    for slab in range(band // SLAB):
        edge = column[slab * SLAB : (slab + 1) * SLAB]
        for tile in range(waves // LANES):
            keep = jnp.where(lane + tile * LANES < edge, 1.0, 0.0).astype(jnp.bfloat16)
            cols = pl.ds(tile * LANES, LANES)
            for t in range(parts):
                value = four_ref[t, pl.ds(slab * SLAB, SLAB), cols] * keep
                if slab < 4:
                    start = t * LANES + lax.rem(slab + turn, 4) * SLAB
                    main[pl.ds(pl.multiple_of(start, SLAB), SLAB), cols] = value
                else:
                    tail[pl.ds(t * SLAB, SLAB), cols] = value

    def picked(k, rows):
        return lax.dot_general(
            table[k], rows[:, half * k : half * (k + 1)], NT, preferred_element_type=jnp.float32
        )

    for n in range(parts // 2):
        rows = main[pl.ds(2 * LANES * n, 2 * LANES), :]
        for k in range(2):
            value = picked(k, rows)
            for s in range(slots):
                for h in range(2):
                    start = 16 * s + 8 * k + 2 * n + h
                    wide[pl.ds(start, owners, stride=CHUNK), :] = value[
                        s * owners : (s + 1) * owners, h * LANES : (h + 1) * LANES
                    ]

    lane = lax.broadcasted_iota(jnp.int32, (owners, LANES), 1)
    rows = tail[...]
    values = [picked(k, rows) for k in range(2)]

    def turned(k, s, h, by):
        value = values[k][s * owners : (s + 1) * owners, h * LANES : (h + 1) * LANES]
        by = (by * SLAB) % LANES
        return pltpu.roll(value, by, 1) if by else value

    for h in range(2):
        for part in range(4):
            for k in range(2):
                out = turned(k, 3, h, 3 - part)
                for s in (2, 1, 0):
                    out = jnp.where(lane < SLAB * (s + 1), turned(k, s, h, s - part), out)
                start = 16 * slots + 8 * k + 4 * h + part
                wide[pl.ds(start, owners, stride=CHUNK), :] = out
            out = jnp.where(lane < SLAB, turned(0, 4, h, -part), turned(1, 4, h, 1 - part))
            start = 16 * slots + 16 + 4 * h + part
            wide[pl.ds(start, owners, stride=CHUNK), :] = out

    block = 16 * CHUNK

    def pack(i, carry):
        rows = pl.ds(pl.multiple_of(i * block, block), block)
        out_ref[rows, :] = wide[rows, :].astype(jnp.bfloat16)
        return carry

    lax.fori_loop(0, owners * CHUNK // block, pack, 0)


def sum_kernel(pair_ref, got_ref, leg_ref, out_ref, leg, both, rows64, out, leg_sem, out_sem):
    slots, count, loops = leg_ref.shape
    waves = 2 * pair_ref.shape[0]
    half = waves // 2
    groups = loops // (5 * LANES)
    peers = got_ref.shape[0] // CHUNK
    levs = peers // (8 * groups)
    south = peers // 2 * CHUNK
    owner = lax.axis_index("lat") * lax.axis_size("lev") + lax.axis_index("lev")

    fetches = [pltpu.make_async_copy(leg_ref.at[s], leg.at[s], leg_sem.at[s]) for s in range(slots)]
    for fetch in fetches:
        fetch.start()

    lane = lax.broadcasted_iota(jnp.int32, (16, LANES), 1)
    signs = (1.0, -1.0)

    def pair_of(src, start, size):
        rows = pl.ds(src * CHUNK + start, size)
        north = got_ref[rows, :].astype(jnp.float32)
        rows = pl.ds(src * CHUNK + south + start, size)
        return north, got_ref[rows, :].astype(jnp.float32)

    def combined(pair):
        return pair[0] + pair[1], pair[0] - pair[1]

    def turned(value, by):
        by = (by * SLAB) % LANES
        return pltpu.roll(value, by, 1) if by else value

    for s in range(slots):
        for j in range(levs):
            for g in range(groups):
                mains, tails = [], []
                for b in range(4):
                    src = (4 * g + b) * levs + j
                    mains.append(combined(pair_of(src, 16 * s, 16)))
                    if s < 4:
                        ends = combined(pair_of(src, 16 * slots, 16))
                        tails.append([turned(e, b - s) for e in ends])
                    else:
                        ends = combined(pair_of(src, 16 * slots + 16, 8))
                        tails.append([jnp.concatenate([turned(e, b), turned(e, b - 1)], 0) for e in ends])
                for p in range(2):
                    m = [x[p] for x in mains]
                    e = [x[p] for x in tails]
                    tiles = (
                        m[0],
                        jnp.where(lane < 32, e[0], m[1]),
                        jnp.where(lane < 32, m[1], jnp.where(lane < 64, e[1], m[2])),
                        jnp.where(lane < 64, m[2], jnp.where(lane < 96, e[2], m[3])),
                        jnp.where(lane < 96, m[3], e[3]),
                    )
                    for i, tile in enumerate(tiles):
                        cols = pl.ds((5 * g + i) * LANES, LANES)
                        both[p, pl.ds(16 * j, 16), cols] = tile.astype(jnp.bfloat16)

        fetches[s].wait()
        dot = functools.partial(lax.dot_general, dimension_numbers=NT, preferred_element_type=jnp.float32)
        sym = dot(both[0], leg[s, pl.ds(0, half), :])
        anti = dot(both[1], leg[s, pl.ds(half, count - half), :])
        middle = dot(both[0], leg[s, pl.ds(half, 16), :])

        low = pair_ref[owner * slots + s]
        sym_limit = lax.shift_right_logical(waves - low + 1, 1)
        anti_limit = lax.shift_right_logical(waves - low, 1) + half + 1
        for j in range(levs):
            a, b = pl.ds(16 * j, 8), pl.ds(16 * j + 8, 8)
            first = slice(16 * j, 16 * j + 8)
            second = slice(16 * j + 8, 16 * j + 16)
            tiles = half // LANES
            for i in range(tiles):
                at = lax.broadcasted_iota(jnp.int32, (8, LANES), 1) + i * LANES
                cols = slice(i * LANES, (i + 1) * LANES)
                rows64[i, pl.ds(8 * j, 8), :] = jnp.where(at < sym_limit, sym[first, cols], sym[second, cols])
            for i in range(tiles + 1):
                width = min(LANES, count - half - i * LANES)
                at = lax.broadcasted_iota(jnp.int32, (8, width), 1) + half + i * LANES
                cols = slice(i * LANES, i * LANES + width)
                value = jnp.where(at < anti_limit, anti[first, cols], anti[second, cols])
                if i == 0:
                    mid = jnp.where(half < sym_limit, middle[first, :1], middle[second, :1])
                    value = jnp.where(at == half, mid, value)
                rows64[tiles + i, pl.ds(8 * j, 8), :width] = value
        for i in range(rows64.shape[0]):
            width = min(LANES, count - i * LANES)
            for c in range(2):
                for v in range(levs // 2):
                    value = rows64[i, pl.ds(16 * v + c, 8, stride=2), :]
                    out[s, pl.ds(4 * levs * c + 8 * v, 8), pl.ds(i * LANES, width)] = value[:, :width]
        pltpu.make_async_copy(out.at[s], out_ref.at[s], out_sem.at[s]).start()
    for s in range(slots):
        pltpu.make_async_copy(out.at[s], out_ref.at[s], out_sem.at[s]).wait()


def shards(fourier, loop_len, pair_m, legendre):
    levels, parts, band, waves = fourier.shape
    slots, count, loops = legendre.shape
    owners = pair_m.shape[0] // slots
    half = waves // 2
    bands = loops // band
    vmem = pl.BlockSpec(memory_space=pltpu.VMEM)
    lengths = jnp.pad(loop_len.reshape(bands, band), ((0, 0), (0, 2 * LANES - band)))
    outgoing = pl.pallas_call(
        pick_kernel,
        out_shape=jax.ShapeDtypeStruct((owners * CHUNK, LANES), jnp.bfloat16),
        in_specs=[vmem] * 3,
        out_specs=vmem,
        scratch_shapes=[
            pltpu.VMEM((2, owners * slots, half), jnp.bfloat16),
            pltpu.VMEM((levels * parts * LANES, waves), jnp.bfloat16),
            pltpu.VMEM((levels * parts * SLAB, waves), jnp.bfloat16),
            pltpu.VMEM((owners * CHUNK, LANES), jnp.float32),
        ],
        compiler_params=pltpu.CompilerParams(vmem_limit_bytes=50 * 2**20),
        name="pick",
    )(pair_m.reshape(owners, slots), lengths, fourier.reshape(levels * parts, band, waves))
    arrived = lax.all_to_all(
        outgoing.reshape(owners, CHUNK, LANES), ("lat", "lev"), split_axis=0, concat_axis=0, tiled=True
    )
    out = pl.pallas_call(
        sum_kernel,
        out_shape=jax.ShapeDtypeStruct((slots, 64, count), jnp.float32),
        in_specs=[
            pl.BlockSpec(memory_space=pltpu.SMEM),
            vmem,
            pl.BlockSpec(memory_space=pl.ANY),
        ],
        out_specs=pl.BlockSpec(memory_space=pl.ANY),
        scratch_shapes=[
            pltpu.VMEM((slots, count, loops), jnp.bfloat16),
            pltpu.VMEM((2, 128, loops), jnp.bfloat16),
            pltpu.VMEM((count // LANES + 1, 64, LANES), jnp.float32),
            pltpu.VMEM((slots, 64, count), jnp.float32),
            pltpu.SemaphoreType.DMA((slots,)),
            pltpu.SemaphoreType.DMA((slots,)),
        ],
        compiler_params=pltpu.CompilerParams(vmem_limit_bytes=50 * 2**20),
        name="transform",
    )(pair_m, arrived.reshape(owners * CHUNK, LANES), legendre)
    return jnp.transpose(out, (0, 2, 1))


def solution(mesh):
    return jax.shard_map(
        shards,
        mesh=mesh,
        in_specs=(P("lev", None, "lat", None), P(), P(), P(("lat", "lev"), None, None)),
        out_specs=P(("lat", "lev"), None, None),
        check_vma=False,
    )
```

time: 165 us -> 76.8 us (0.47)
  waiting for transfers between devices: 74.8 us -> 0 us
  blocking collectives: 0 us -> 55.7 us
  local copies, waits for them, and re-layouts: 48.4 us -> 3.58 us
  matrix products: 17.3 us -> 0 us
  Pallas kernels: 0 us -> 17.1 us
  starting transfers between devices: 15.7 us -> 0 us
  other arithmetic: 7.78 us -> 0 us
    all_to_all x0 -> x1, blocking collectives: none -> 55.7 us  [shards(): lax.all_to_all(outgoing.reshape(owners, CHUNK, LANES), ('lat', 'lev'), sp...]
    all_to_all x1 -> x0, waiting for transfers between devices: 42.4 us -> none  [shards(): lax.all_to_all(outgoing, ('lat', 'lev'), split_axis=0, concat_axis=6, til...]
    ppermute x1 -> x0, waiting for transfers between devices: 32.4 us -> none  [swapped(): return lax.ppermute(value, axis, pairs)]
    unnamed x7 -> x4, local copies, waits for them, and re-layouts: 22.6 us -> 1.93 us
    dot_general x3 -> x0, matrix products: 17.3 us -> none  [the longest x1 9.22 us: shards(): jnp.einsum(einsum_form, table[:, sym_rows:], anti_data, preferred_element...]
    pallas_call x0 -> x2, Pallas kernels: none -> 17.1 us  [the longest x1 10.2 us: shards(): pl.pallas_call(sum_kernel, out_shape=jax.ShapeDtypeStruct((slots, 64, cou...]
    all_to_all x1 -> x0, starting transfers between devices: 12 us -> none  [shards(): lax.all_to_all(outgoing, ('lat', 'lev'), split_axis=0, concat_axis=6, til...]
    convert_element_type x1 -> x0, local copies, waits for them, and re-layouts: 9.62 us -> none  [shards(): picked = jnp.einsum('qm,gdcrm->qgdcr', selector, stacked, preferred_eleme...]
  transfers between devices with their start and end apart: 2 -> 0, of which waited for: 2 -> 0; matrix products, arithmetic and copies ran while one was open for 16% -> 0% of each run, Pallas kernels for 0% -> 0%
where the time goes in v1:
time: 76.8 us; the launch traced here: 76.5 us
  blocking collectives  55.7 us (73%)
  Pallas kernels  17.1 us (22%)
  local copies, waits for them, and re-layouts  3.58 us (5%)
    all_to_all x1, blocking collectives, shards(): lax.all_to_all(outgoing.reshape(owners, CHUNK, LANES), ('lat', 'lev'), sp...  55.7 us
    pallas_call x1, Pallas kernels, shards(): pl.pallas_call(sum_kernel, out_shape=jax.ShapeDtypeStruct((slots, 64, cou...  10.2 us
    pallas_call x1, Pallas kernels, shards(): pl.pallas_call(pick_kernel, out_shape=jax.ShapeDtypeStruct((owners * CHUN...  6.94 us
    unnamed x4, local copies, waits for them, and re-layouts  1.93 us

profile of v1, /device:TPU:1, one launch (start us, length us, event | category | flops | bytes accessed | tf_op | source)
XLA Modules:
  0.0 76.5 jit_solution(9404490287391653966)
XLA Ops:
  0.0 0.8 %reshape.16 = s32[8,160]{1,0:T(8,128)S(1)} reshape(s32[1280]{0:T(1024)} %param.5) | data formatting | bytes 10240 | tf_op jit(solution)/shard_map/reshape | solution.py:196
  0.8 0.9 %reshape.15.pair_ref = s32[128,5]{1,0:T(8,128)S(1)} reshape(s32[640]{0:T(1024)} %pair_ref.1) | data formatting | bytes 5120 | tf_op jit(solution)/shard_map/reshape | solution.py:210
  1.7 0.0 copy-start
  1.7 1.9 %copy-done = bf16[4,2,160,1280]{3,2,1,0:T(8,128)(2,1)S(1)} copy-done((bf16[4,2,160,1280]{3,2,1,0:T(8,128)(2,1)S(1)}, bf16[4,2,160,1280]{3,2,1,0:T(8,128)(2,1)}, u32[]{:S(2)}) %copy-start) | copy-done | bytes 3276824
  3.6 6.9 %pick.1 = bf16[13312,128]{1,0:T(8,128)(2,1)} custom-call(s32[128,5]{1,0:T(8,128)S(1)} %reshape.15.pair_ref, s32[8,256]{1,0:T(8,128)S(1)} %pad.4.len_ref, bf16[8,160,1280]{2,1,0:T(8,128)(2,1)S(1)} %bitcast.5), custom_call_target="tpu_custom_call" | custom-call | tf_op jit(solution)/shard_map/pick/pallas_call | solution.py:197
  10.5 0.0 copy-start.1
  10.5 55.7 %all_to_all.5 = bf16[128,104,128]{2,1,0:T(8,128)(2,1)S(1)} all-to-all(bf16[128,104,128]{2,1,0:T(8,128)(2,1)} %bitcast.6), channel_id=1, replica_groups=mesh['lat'=16,'lev'=8] {'lat','lev'}, dimensions={0} | all-to-all | bytes 6815744 | tf_op jit(solution)/shard_map/all_to_all | solution.py:211
  66.3 0.0 copy-done.1
  66.3 10.2 %transform.1 = f32[5,64,1281]{2,1,0:T(8,128)} custom-call(s32[640]{0:T(1024)S(1)} %copy-done.1, bf16[13312,128]{1,0:T(8,128)(2,1)S(1)} %bitcast.4, bf16[5,1281,1280]{2,1,0:T(8,128)(2,1)} %leg_ref.1), custom_call_target="tpu_custom_call" | custom-call | tf_op jit(solution)/shard_map/transform/pallas_call | solution.py:214
  (1 shorter events, 0.0 us)
Async XLA Ops:
  1.7 1.9 %copy-start = (bf16[4,2,160,1280]{3,2,1,0:T(8,128)(2,1)S(1)}, bf16[4,2,160,1280]{3,2,1,0:T(8,128)(2,1)}, u32[]{:S(2)}) copy-start(bf16[4,2,160,1280]{3,2,1,0:T(8,128)(2,1)} %param.4) | copy-start | bytes 9830404
  10.5 55.8 %copy-start.1 = (s32[640]{0:T(1024)S(1)}, s32[640]{0:T(1024)}, u32[]{:S(2)}) copy-start(s32[640]{0:T(1024)} %pair_ref.1) | copy-start | bytes 7684

commit v2 on v1

--- a/solution.py
+++ b/solution.py
@@ -13,31 +13,57 @@
 NT = (((1,), (1,)), ((), ()))
 
 
-def pick_kernel(pair_ref, len_ref, four_ref, out_ref, table, main, tail, wide):
+def pick_kernel(
+    pair_hbm, len_hbm, four_ref, leg_ref, out_ref, held_ref, pair_ref, len_ref, four, column, lows, table, main, tail, wide, sems
+):
     parts, band, waves = four_ref.shape
     half = waves // 2
-    owners, slots = pair_ref.shape
-    bands = len_ref.shape[0]
-    place = lax.rem(lax.axis_index("lat"), bands)
+    slots = held_ref.shape[0]
+    owners = pair_ref.shape[0] * LANES // slots
+    place = lax.rem(lax.axis_index("lat"), len_ref.shape[0] * LANES // band)
     turn = lax.rem(place, 4)
 
-    lane = lax.broadcasted_iota(jnp.int32, (owners, half), 1)
+    small = [
+        pltpu.make_async_copy(pair_hbm, pair_ref, sems.at[parts + slots]),
+        pltpu.make_async_copy(len_hbm, len_ref, sems.at[parts + slots + 1]),
+    ]
+    fetches = [pltpu.make_async_copy(four_ref.at[t], four.at[t], sems.at[t]) for t in range(parts)]
+    fetches += [
+        pltpu.make_async_copy(leg_ref.at[s], held_ref.at[s], sems.at[parts + s]) for s in range(slots)
+    ]
+    for fetch in small + fetches:
+        fetch.start()
+    for fetch in small:
+        fetch.wait()
+
+    def column_of(row):
+        return jnp.transpose(jnp.broadcast_to(row, (LANES, LANES)))
+
+    for n in range(pair_ref.shape[0]):
+        lows[pl.ds(n * LANES, LANES), :] = column_of(pair_ref[pl.ds(n, 1), :])
     for s in range(slots):
-        low = pair_ref[:, s : s + 1]
+        low = lows[pl.ds(s, owners, stride=slots), :]
         rows = pl.ds(s * owners, owners)
-        table[0, rows, :] = jnp.where(lane == low, 1.0, 0.0).astype(jnp.bfloat16)
-        table[1, rows, :] = jnp.where(lane == half - 1 - low, 1.0, 0.0).astype(jnp.bfloat16)
-
-    limit = jnp.minimum(waves, lax.shift_right_logical(len_ref[pl.ds(place, 1), :], 1))
-    column = jnp.transpose(jnp.broadcast_to(limit, (LANES, limit.shape[1])))
+        for tile in range(half // LANES):
+            lane = lax.broadcasted_iota(jnp.int32, (owners, LANES), 1) + tile * LANES
+            cols = pl.ds(tile * LANES, LANES)
+            table[0, rows, cols] = jnp.where(lane == low, 1.0, 0.0).astype(jnp.bfloat16)
+            table[1, rows, cols] = jnp.where(lane == half - 1 - low, 1.0, 0.0).astype(jnp.bfloat16)
+
+    first = lax.div(place * band, LANES)
+    for n in range(2):
+        limit = jnp.minimum(waves, lax.shift_right_logical(len_ref[pl.ds(first + n, 1), :], 1))
+        column[pl.ds(n * LANES, LANES), :] = column_of(limit)
     lane = lax.broadcasted_iota(jnp.int32, (SLAB, LANES), 1)
+    for t in range(parts):
+        fetches[t].wait()
     for slab in range(band // SLAB):
-        edge = column[slab * SLAB : (slab + 1) * SLAB]
+        edge = column[pl.ds(pl.multiple_of((turn + slab) * SLAB, SLAB), SLAB), :]
         for tile in range(waves // LANES):
             keep = jnp.where(lane + tile * LANES < edge, 1.0, 0.0).astype(jnp.bfloat16)
             cols = pl.ds(tile * LANES, LANES)
             for t in range(parts):
-                value = four_ref[t, pl.ds(slab * SLAB, SLAB), cols] * keep
+                value = four[t, pl.ds(slab * SLAB, SLAB), cols] * keep
                 if slab < 4:
                     start = t * LANES + lax.rem(slab + turn, 4) * SLAB
                     main[pl.ds(pl.multiple_of(start, SLAB), SLAB), cols] = value
@@ -89,10 +115,12 @@
         return carry
 
     lax.fori_loop(0, owners * CHUNK // block, pack, 0)
-
-
-def sum_kernel(pair_ref, got_ref, leg_ref, out_ref, leg, both, rows64, out, leg_sem, out_sem):
-    slots, count, loops = leg_ref.shape
+    for fetch in fetches[parts:]:
+        fetch.wait()
+
+
+def sum_kernel(pair_ref, got_ref, leg, out_ref, both, rows64, out, out_sem):
+    slots, count, loops = leg.shape
     waves = 2 * pair_ref.shape[0]
     half = waves // 2
     groups = loops // (5 * LANES)
@@ -101,12 +129,7 @@
     south = peers // 2 * CHUNK
     owner = lax.axis_index("lat") * lax.axis_size("lev") + lax.axis_index("lev")
 
-    fetches = [pltpu.make_async_copy(leg_ref.at[s], leg.at[s], leg_sem.at[s]) for s in range(slots)]
-    for fetch in fetches:
-        fetch.start()
-
     lane = lax.broadcasted_iota(jnp.int32, (16, LANES), 1)
-    signs = (1.0, -1.0)
 
     def pair_of(src, start, size):
         rows = pl.ds(src * CHUNK + start, size)
@@ -148,7 +171,6 @@
                         cols = pl.ds((5 * g + i) * LANES, LANES)
                         both[p, pl.ds(16 * j, 16), cols] = tile.astype(jnp.bfloat16)
 
-        fetches[s].wait()
         dot = functools.partial(lax.dot_general, dimension_numbers=NT, preferred_element_type=jnp.float32)
         sym = dot(both[0], leg[s, pl.ds(0, half), :])
         anti = dot(both[1], leg[s, pl.ds(half, count - half), :])
@@ -158,7 +180,6 @@
         sym_limit = lax.shift_right_logical(waves - low + 1, 1)
         anti_limit = lax.shift_right_logical(waves - low, 1) + half + 1
         for j in range(levs):
-            a, b = pl.ds(16 * j, 8), pl.ds(16 * j + 8, 8)
             first = slice(16 * j, 16 * j + 8)
             second = slice(16 * j + 8, 16 * j + 16)
             tiles = half // LANES
@@ -186,28 +207,45 @@
         pltpu.make_async_copy(out.at[s], out_ref.at[s], out_sem.at[s]).wait()
 
 
+def in_hbm(value):
+    return pltpu.with_memory_space_constraint(value, pltpu.HBM)
+
+
 def shards(fourier, loop_len, pair_m, legendre):
     levels, parts, band, waves = fourier.shape
     slots, count, loops = legendre.shape
     owners = pair_m.shape[0] // slots
     half = waves // 2
-    bands = loops // band
     vmem = pl.BlockSpec(memory_space=pltpu.VMEM)
-    lengths = jnp.pad(loop_len.reshape(bands, band), ((0, 0), (0, 2 * LANES - band)))
-    outgoing = pl.pallas_call(
+    hbm = pl.BlockSpec(memory_space=pltpu.HBM)
+    outgoing, held = pl.pallas_call(
         pick_kernel,
-        out_shape=jax.ShapeDtypeStruct((owners * CHUNK, LANES), jnp.bfloat16),
-        in_specs=[vmem] * 3,
-        out_specs=vmem,
+        out_shape=(
+            jax.ShapeDtypeStruct((owners * CHUNK, LANES), jnp.bfloat16),
+            pltpu.VMEM(legendre.shape, legendre.dtype),
+        ),
+        in_specs=[hbm] * 4,
+        out_specs=(vmem, vmem),
         scratch_shapes=[
+            pltpu.VMEM((owners * slots // LANES, LANES), jnp.int32),
+            pltpu.VMEM((loops // LANES, LANES), jnp.int32),
+            pltpu.VMEM((levels * parts, band, waves), jnp.bfloat16),
+            pltpu.VMEM((2 * LANES, LANES), jnp.int32),
+            pltpu.VMEM((owners * slots, LANES), jnp.int32),
             pltpu.VMEM((2, owners * slots, half), jnp.bfloat16),
             pltpu.VMEM((levels * parts * LANES, waves), jnp.bfloat16),
             pltpu.VMEM((levels * parts * SLAB, waves), jnp.bfloat16),
             pltpu.VMEM((owners * CHUNK, LANES), jnp.float32),
+            pltpu.SemaphoreType.DMA((levels * parts + slots + 2,)),
         ],
-        compiler_params=pltpu.CompilerParams(vmem_limit_bytes=50 * 2**20),
+        compiler_params=pltpu.CompilerParams(vmem_limit_bytes=32 * 2**20),
         name="pick",
-    )(pair_m.reshape(owners, slots), lengths, fourier.reshape(levels * parts, band, waves))
+    )(
+        in_hbm(pair_m.reshape(-1, LANES)),
+        in_hbm(loop_len.reshape(-1, LANES)),
+        in_hbm(fourier.reshape(levels * parts, band, waves)),
+        in_hbm(legendre),
+    )
     arrived = lax.all_to_all(
         outgoing.reshape(owners, CHUNK, LANES), ("lat", "lev"), split_axis=0, concat_axis=0, tiled=True
     )
@@ -217,20 +255,18 @@
         in_specs=[
             pl.BlockSpec(memory_space=pltpu.SMEM),
             vmem,
-            pl.BlockSpec(memory_space=pl.ANY),
+            vmem,
         ],
         out_specs=pl.BlockSpec(memory_space=pl.ANY),
         scratch_shapes=[
-            pltpu.VMEM((slots, count, loops), jnp.bfloat16),
             pltpu.VMEM((2, 128, loops), jnp.bfloat16),
             pltpu.VMEM((count // LANES + 1, 64, LANES), jnp.float32),
             pltpu.VMEM((slots, 64, count), jnp.float32),
             pltpu.SemaphoreType.DMA((slots,)),
-            pltpu.SemaphoreType.DMA((slots,)),
         ],
-        compiler_params=pltpu.CompilerParams(vmem_limit_bytes=50 * 2**20),
+        compiler_params=pltpu.CompilerParams(vmem_limit_bytes=16 * 2**20),
         name="transform",
-    )(pair_m, arrived.reshape(owners * CHUNK, LANES), legendre)
+    )(pair_m, arrived.reshape(owners * CHUNK, LANES), held)
     return jnp.transpose(out, (0, 2, 1))
 
 

time: 76.8 us -> 70.1 us (0.913)
  local copies, waits for them, and re-layouts: 3.58 us -> 0.01 us
  Pallas kernels: 17.1 us -> 14.3 us
    pallas_call x1, Pallas kernels: 10.2 us -> 7.48 us  [shards(): pl.pallas_call(sum_kernel, out_shape=jax.ShapeDtypeStruct((slots, 64, cou...]
    unnamed x4 -> x2, local copies, waits for them, and re-layouts: 1.93 us -> 0.01 us
    reshape x2 -> x0, local copies, waits for them, and re-layouts: 1.65 us -> none  [the longest x1 0.88 us: shards(): pair_m.reshape(owners, slots)]
where the time goes in v2:
time: 70.1 us; the launch traced here: 69.9 us
  blocking collectives  55.5 us (79%)
  Pallas kernels  14.3 us (20%)
    all_to_all x1, blocking collectives, shards(): lax.all_to_all(outgoing.reshape(owners, CHUNK, LANES), ('lat', 'lev'), sp...  55.5 us
    pallas_call x1, Pallas kernels, shards(): pl.pallas_call(sum_kernel, out_shape=jax.ShapeDtypeStruct((slots, 64, cou...  7.48 us
    pallas_call x1, Pallas kernels, shards(): pl.pallas_call(pick_kernel, out_shape=(jax.ShapeDtypeStruct((owners * CHU...  6.86 us

profile of v2, /device:TPU:1, one launch (start us, length us, event | category | flops | bytes accessed | tf_op | source)
XLA Modules:
  0.0 69.9 jit_solution(2352868270154730865)
XLA Ops:
  0.0 6.9 %pick.1 = (bf16[13312,128]{1,0:T(8,128)(2,1)S(1)}, bf16[5,1281,1280]{2,1,0:T(8,128)(2,1)S(1)}) custom-call(s32[5,128]{1,0:T(8,128)} %bitcast.8, s32[10,128]{1,0:T(8,128)} %bitcast.10, bf16[8,160,1280]{2,1,0:T(8,128)(2,1)} %bitcast.9, bf16[5,1281,1280]{2,1,0:T(8,128)(2,1)} %leg_ref.1), custom_call_target="tpu_custom_call" | custom-call | tf_op jit(solution)/shard_map/pick/pallas_call | solution.py:221
  6.9 0.0 copy-start
  6.9 55.5 %all_to_all.5 = bf16[128,104,128]{2,1,0:T(8,128)(2,1)S(1)} all-to-all(bf16[128,104,128]{2,1,0:T(8,128)(2,1)S(1)} %bitcast.7), channel_id=1, replica_groups=mesh['lat'=16,'lev'=8] {'lat','lev'}, dimensions={0} | all-to-all | bytes 6815744 | tf_op jit(solution)/shard_map/all_to_all | solution.py:249
  62.4 0.0 copy-done
  62.4 7.5 %transform.1 = f32[5,64,1281]{2,1,0:T(8,128)} custom-call(s32[640]{0:T(1024)S(1)} %copy-done, bf16[13312,128]{1,0:T(8,128)(2,1)S(1)} %bitcast.6, bf16[5,1281,1280]{2,1,0:T(8,128)(2,1)S(1)} %get-tuple-element.8.leg), custom_call_target="tpu_custom_call" | custom-call | tf_op jit(solution)/shard_map/transform/pallas_call | solution.py:252
Async XLA Ops:
  6.9 55.6 %copy-start = (s32[640]{0:T(1024)S(1)}, s32[640]{0:T(1024)}, u32[]{:S(2)}) copy-start(s32[640]{0:T(1024)} %pair_ref.1) | copy-start | bytes 7684

commit v3 on v2

v3 whole, which is shorter than its diff:
```python
import functools

import jax
import jax.numpy as jnp
from jax import lax
from jax.experimental import pallas as pl
from jax.experimental.pallas import tpu as pltpu
from jax.sharding import PartitionSpec as P

LANES = 128
SLAB = 32
CHUNK = 104
HELD = 3
NT = (((1,), (1,)), ((), ()))


def pick_kernel(
    pair_hbm, len_hbm, four_ref, leg_ref, out_ref, held_ref, pair_ref, len_ref, four, column, lows, table, keep, mains, tails, wide, sems
):
    parts, band, waves = four_ref.shape
    half = waves // 2
    slots = leg_ref.shape[0]
    owners = pair_ref.shape[0] * LANES // slots
    place = lax.rem(lax.axis_index("lat"), len_ref.shape[0] * LANES // band)
    turn = lax.rem(place, 4)

    small = [
        pltpu.make_async_copy(pair_hbm, pair_ref, sems.at[parts + slots]),
        pltpu.make_async_copy(len_hbm, len_ref, sems.at[parts + slots + 1]),
    ]
    fetches = [pltpu.make_async_copy(four_ref.at[t], four.at[t], sems.at[t]) for t in range(parts)]
    holds = [
        pltpu.make_async_copy(leg_ref.at[s], held_ref.at[s], sems.at[parts + s]) for s in range(HELD)
    ]
    for copy in small + fetches + holds:
        copy.start()
    for copy in small:
        copy.wait()

    def column_of(row):
        return jnp.transpose(jnp.broadcast_to(row, (LANES, LANES)))

    first = lax.div(place * band, LANES)
    for n in range(2):
        limit = jnp.minimum(waves, lax.shift_right_logical(len_ref[pl.ds(first + n, 1), :], 1))
        column[pl.ds(n * LANES, LANES), :] = column_of(limit)
    for n in range(pair_ref.shape[0]):
        lows[pl.ds(n * LANES, LANES), :] = column_of(pair_ref[pl.ds(n, 1), :])
    lane = lax.broadcasted_iota(jnp.int32, (SLAB, LANES), 1)
    for slab in range(band // SLAB):
        edge = column[pl.ds(pl.multiple_of((turn + slab) * SLAB, SLAB), SLAB), :]
        for tile in range(waves // LANES):
            inside = jnp.where(lane + tile * LANES < edge, 1.0, 0.0).astype(jnp.bfloat16)
            keep[pl.ds(slab * SLAB, SLAB), pl.ds(tile * LANES, LANES)] = inside
    lane = lax.broadcasted_iota(jnp.int32, (owners, LANES), 1)
    for s in range(slots):
        low = lows[pl.ds(s, owners, stride=slots), :]
        rows = pl.ds(s * owners, owners)
        for tile in range(half // LANES):
            wave = lane + tile * LANES
            cols = pl.ds(tile * LANES, LANES)
            table[0, rows, cols] = jnp.where(wave == low, 1.0, 0.0).astype(jnp.bfloat16)
            table[1, rows, cols] = jnp.where(wave == half - 1 - low, 1.0, 0.0).astype(jnp.bfloat16)

    def mask(n):
        for h in range(2):
            t = 2 * n + h
            for slab in range(band // SLAB):
                rows = pl.ds(slab * SLAB, SLAB)
                value = four[t, rows, :] * keep[rows, :]
                if slab < 4:
                    start = h * LANES + lax.rem(slab + turn, 4) * SLAB
                    mains[n][pl.ds(pl.multiple_of(start, SLAB), SLAB), :] = value
                else:
                    tails[pl.ds(t * SLAB, SLAB), :] = value

    def picked(k, rows):
        return lax.dot_general(
            table[k], rows[:, half * k : half * (k + 1)], NT, preferred_element_type=jnp.float32
        )

    def wait(n):
        fetches[2 * n].wait()
        fetches[2 * n + 1].wait()

    def place_main(n):
        rows = mains[n][...]
        for k in range(2):
            value = picked(k, rows)
            for s in range(slots):
                for h in range(2):
                    start = 16 * s + 8 * k + 2 * n + h
                    wide[pl.ds(start, owners, stride=CHUNK), :] = value[
                        s * owners : (s + 1) * owners, h * LANES : (h + 1) * LANES
                    ]

    for n in range(parts // 2):
        wait(n)
        mask(n)
    lane = lax.broadcasted_iota(jnp.int32, (owners, LANES), 1)
    rows = tails[...]
    values = [picked(k, rows) for k in range(2)]
    place_main(0)

    def piece(k, s, h):
        return values[k][s * owners : (s + 1) * owners, h * LANES : (h + 1) * LANES]

    def exchange(x, y, apart):
        low = (lane & (apart * SLAB)) == 0
        back = LANES - apart * SLAB
        return (
            jnp.where(low, x, pltpu.roll(y, apart * SLAB, 1)),
            jnp.where(low, pltpu.roll(x, back, 1), y),
        )

    for h in range(2):
        for k in range(2):
            v = [piece(k, s, h) for s in range(4)]
            v[0], v[2] = exchange(v[0], v[2], 2)
            v[1], v[3] = exchange(v[1], v[3], 2)
            v[0], v[1] = exchange(v[0], v[1], 1)
            v[2], v[3] = exchange(v[2], v[3], 1)
            for part in range(4):
                start = 16 * slots + 8 * k + 4 * h + part
                wide[pl.ds(start, owners, stride=CHUNK), :] = v[part]
        place_main(1 + h)
        lower, upper = piece(0, 4, h), pltpu.roll(piece(1, 4, h), SLAB, 1)
        for part in range(4):
            out = jnp.where((lane & (3 * SLAB)) == part * SLAB, lower, upper)
            if part:
                out = pltpu.roll(out, LANES - part * SLAB, 1)
            start = 16 * slots + 16 + 4 * h + part
            wide[pl.ds(start, owners, stride=CHUNK), :] = out

    place_main(3)
    block = 16 * CHUNK

    def pack(i, carry):
        rows = pl.ds(pl.multiple_of(i * block, block), block)
        out_ref[rows, :] = wide[rows, :].astype(jnp.bfloat16)
        return carry

    lax.fori_loop(0, owners * CHUNK // block, pack, 0)
    for copy in holds:
        copy.wait()


def sum_kernel(pair_ref, got_ref, held_ref, leg_ref, out_ref, rest, both, rows64, out, leg_sem, out_sem):
    slots, count, loops = leg_ref.shape
    waves = 2 * pair_ref.shape[0]
    half = waves // 2
    groups = loops // (5 * LANES)
    peers = got_ref.shape[0] // CHUNK
    levs = peers // (8 * groups)
    south = peers // 2 * CHUNK
    owner = lax.axis_index("lat") * lax.axis_size("lev") + lax.axis_index("lev")

    fetches = [pltpu.make_async_copy(leg_ref.at[s], rest.at[s - HELD], leg_sem.at[s]) for s in range(HELD, slots)]
    for fetch in fetches:
        fetch.start()

    lane = lax.broadcasted_iota(jnp.int32, (16, LANES), 1)

    def pair_of(src, start, size):
        rows = pl.ds(src * CHUNK + start, size)
        north = got_ref[rows, :].astype(jnp.float32)
        rows = pl.ds(src * CHUNK + south + start, size)
        return north, got_ref[rows, :].astype(jnp.float32)

    def combined(pair):
        return pair[0] + pair[1], pair[0] - pair[1]

    def turned(value, by):
        by = (by * SLAB) % LANES
        return pltpu.roll(value, by, 1) if by else value

    def build(s):
        for j in range(levs):
            for g in range(groups):
                mains, tails = [], []
                for b in range(4):
                    src = (4 * g + b) * levs + j
                    mains.append(combined(pair_of(src, 16 * s, 16)))
                    if s < 4:
                        ends = combined(pair_of(src, 16 * slots, 16))
                        tails.append([turned(e, b - s) for e in ends])
                    else:
                        ends = combined(pair_of(src, 16 * slots + 16, 8))
                        tails.append([jnp.concatenate([turned(e, b), turned(e, b - 1)], 0) for e in ends])
                for p in range(2):
                    m = [x[p] for x in mains]
                    e = [x[p] for x in tails]
                    tiles = (
                        m[0],
                        jnp.where(lane < 32, e[0], m[1]),
                        jnp.where(lane < 32, m[1], jnp.where(lane < 64, e[1], m[2])),
                        jnp.where(lane < 64, m[2], jnp.where(lane < 96, e[2], m[3])),
                        jnp.where(lane < 96, m[3], e[3]),
                    )
                    for i, tile in enumerate(tiles):
                        cols = pl.ds((5 * g + i) * LANES, LANES)
                        both[s][p, pl.ds(16 * j, 16), cols] = tile.astype(jnp.bfloat16)

    tiles = half // LANES
    dot = functools.partial(lax.dot_general, dimension_numbers=NT, preferred_element_type=jnp.float32)

    def sums(s):
        if s >= HELD:
            fetches[s - HELD].wait()
        leg = held_ref.at[s] if s < HELD else rest.at[s - HELD]
        sym = dot(both[s][0], leg[pl.ds(0, half + 16), :])
        anti = dot(both[s][1], leg[pl.ds(half, count - half), :])
        return sym, anti

    def finish(s, sym, anti):
        low = pair_ref[owner * slots + s]
        sym_limit = lax.shift_right_logical(waves - low + 1, 1)
        anti_limit = lax.shift_right_logical(waves - low, 1) + half + 1
        for j in range(levs):
            first = slice(16 * j, 16 * j + 8)
            second = slice(16 * j + 8, 16 * j + 16)
            for i in range(tiles):
                at = lax.broadcasted_iota(jnp.int32, (8, LANES), 1) + i * LANES
                cols = slice(i * LANES, (i + 1) * LANES)
                rows64[s][i, pl.ds(8 * j, 8), :] = jnp.where(at < sym_limit, sym[first, cols], sym[second, cols])
            for i in range(tiles + 1):
                width = min(LANES, count - half - i * LANES)
                at = lax.broadcasted_iota(jnp.int32, (8, width), 1) + half + i * LANES
                cols = slice(i * LANES, i * LANES + width)
                value = jnp.where(at < anti_limit, anti[first, cols], anti[second, cols])
                if i == 0:
                    middle = slice(half, half + 1)
                    mid = jnp.where(half < sym_limit, sym[first, middle], sym[second, middle])
                    value = jnp.where(at == half, mid, value)
                rows64[s][tiles + i, pl.ds(8 * j, 8), :width] = value
        for i in range(2 * tiles + 1):
            width = min(LANES, count - i * LANES)
            for c in range(2):
                for v in range(levs // 2):
                    value = rows64[s][i, pl.ds(16 * v + c, 8, stride=2), :]
                    out[s][pl.ds(4 * levs * c + 8 * v, 8), pl.ds(i * LANES, width)] = value[:, :width]

    copies = [pltpu.make_async_copy(out[s], out_ref.at[s], out_sem.at[s]) for s in range(slots)]
    build(0)
    for s in range(slots):
        total = sums(s)
        if s + 1 < slots:
            build(s + 1)
        finish(s, *total)
        copies[s].start()
    for copy in copies:
        copy.wait()


def in_hbm(value):
    return pltpu.with_memory_space_constraint(value, pltpu.HBM)


def pick(fourier, loop_len, pair_m, legendre):
    levels, parts, band, waves = fourier.shape
    slots, count, loops = legendre.shape
    owners = pair_m.shape[0] // slots
    half = waves // 2
    hbm = pl.BlockSpec(memory_space=pltpu.HBM)
    vmem = pl.BlockSpec(memory_space=pltpu.VMEM)
    return pl.pallas_call(
        pick_kernel,
        out_shape=(
            jax.ShapeDtypeStruct((owners * CHUNK, LANES), jnp.bfloat16),
            pltpu.VMEM((HELD, count, loops), legendre.dtype),
        ),
        in_specs=[hbm] * 4,
        out_specs=(vmem, vmem),
        scratch_shapes=[
            pltpu.VMEM((owners * slots // LANES, LANES), jnp.int32),
            pltpu.VMEM((loops // LANES, LANES), jnp.int32),
            pltpu.VMEM((levels * parts, band, waves), jnp.bfloat16),
            pltpu.VMEM((2 * LANES, LANES), jnp.int32),
            pltpu.VMEM((owners * slots, LANES), jnp.int32),
            pltpu.VMEM((2, owners * slots, half), jnp.bfloat16),
            pltpu.VMEM((band, waves), jnp.bfloat16),
            [pltpu.VMEM((2 * LANES, waves), jnp.bfloat16)] * (levels * parts // 2),
            pltpu.VMEM((levels * parts * SLAB, waves), jnp.bfloat16),
            pltpu.VMEM((owners * CHUNK, LANES), jnp.float32),
            pltpu.SemaphoreType.DMA((levels * parts + slots + 2,)),
        ],
        compiler_params=pltpu.CompilerParams(vmem_limit_bytes=32 * 2**20),
        name="pick",
    )(
        in_hbm(pair_m.reshape(-1, LANES)),
        in_hbm(loop_len.reshape(-1, LANES)),
        in_hbm(fourier.reshape(levels * parts, band, waves)),
        in_hbm(legendre),
    )


def transform(pair_m, arrived, held, legendre):
    slots, count, loops = legendre.shape
    vmem = pl.BlockSpec(memory_space=pltpu.VMEM)
    out = pl.pallas_call(
        sum_kernel,
        out_shape=jax.ShapeDtypeStruct((slots, 64, count), jnp.float32),
        in_specs=[pl.BlockSpec(memory_space=pltpu.SMEM), vmem, vmem, pl.BlockSpec(memory_space=pltpu.HBM)],
        out_specs=pl.BlockSpec(memory_space=pl.ANY),
        scratch_shapes=[
            pltpu.VMEM((slots - HELD, count, loops), jnp.bfloat16),
            [pltpu.VMEM((2, 128, loops), jnp.bfloat16)] * slots,
            [pltpu.VMEM((count // LANES + 1, 64, LANES), jnp.float32)] * slots,
            [pltpu.VMEM((64, count), jnp.float32)] * slots,
            pltpu.SemaphoreType.DMA((slots,)),
            pltpu.SemaphoreType.DMA((slots,)),
        ],
        compiler_params=pltpu.CompilerParams(vmem_limit_bytes=28 * 2**20),
        name="transform",
    )(pair_m, arrived, held, in_hbm(legendre))
    return jnp.transpose(out, (0, 2, 1))


def shards(fourier, loop_len, pair_m, legendre):
    outgoing, held = pick(fourier, loop_len, pair_m, legendre)
    chunks = outgoing.reshape(-1, CHUNK, LANES)
    arrived = lax.all_to_all(chunks, ("lat", "lev"), split_axis=0, concat_axis=0, tiled=True)
    return transform(pair_m, arrived.reshape(-1, LANES), held, legendre)


def solution(mesh):
    return jax.shard_map(
        shards,
        mesh=mesh,
        in_specs=(P("lev", None, "lat", None), P(), P(), P(("lat", "lev"), None, None)),
        out_specs=P(("lat", "lev"), None, None),
        check_vma=False,
    )
```

time: 70.1 us -> 68.7 us (0.980)
  Pallas kernels: 14.3 us -> 13 us
    pallas_call x2, Pallas kernels: 14.3 us -> 13 us  [the longest x1 7.42 us: transform(): pl.pallas_call(sum_kernel, out_shape=jax.ShapeDtypeStruct((slots, 64, cou...]
where the time goes in v3:
time: 68.7 us; the launch traced here: 68.5 us
  blocking collectives  55.6 us (81%)
  Pallas kernels  13 us (19%)
    all_to_all x1, blocking collectives, shards(): lax.all_to_all(chunks, ('lat', 'lev'), split_axis=0, concat_axis=0, tiled...  55.6 us
    pallas_call x1, Pallas kernels, transform(): pl.pallas_call(sum_kernel, out_shape=jax.ShapeDtypeStruct((slots, 64, cou...  7.42 us
    pallas_call x1, Pallas kernels, pick(): pl.pallas_call(pick_kernel, out_shape=(jax.ShapeDtypeStruct((owners * CHU...  5.55 us

profile of v3, /device:TPU:1, one launch (start us, length us, event | category | flops | bytes accessed | tf_op | source)
XLA Modules:
  0.0 68.5 jit_solution(10662668371013965085)
XLA Ops:
  0.0 5.5 %pick.1 = (bf16[13312,128]{1,0:T(8,128)(2,1)S(1)}, bf16[3,1281,1280]{2,1,0:T(8,128)(2,1)S(1)}) custom-call(s32[5,128]{1,0:T(8,128)} %bitcast.8, s32[10,128]{1,0:T(8,128)} %bitcast.10, bf16[8,160,1280]{2,1,0:T(8,128)(2,1)} %bitcast.9, bf16[5,1281,1280]{2,1,0:T(8,128)(2,1)} %leg_ref.3), custom_call_target="tpu_custom_call" | custom-call | tf_op jit(solution)/shard_map/pick/pallas_call | solution.py:266
  5.6 0.0 copy-start
  5.6 55.6 %all_to_all.5 = bf16[128,104,128]{2,1,0:T(8,128)(2,1)S(1)} all-to-all(bf16[128,104,128]{2,1,0:T(8,128)(2,1)S(1)} %bitcast.7), channel_id=1, replica_groups=mesh['lat'=16,'lev'=8] {'lat','lev'}, dimensions={0} | all-to-all | bytes 6815744 | tf_op jit(solution)/shard_map/all_to_all | solution.py:322
  61.1 0.0 copy-done
  61.1 7.4 %transform.1 = f32[5,64,1281]{2,1,0:T(8,128)} custom-call(s32[640]{0:T(1024)S(1)} %copy-done, bf16[13312,128]{1,0:T(8,128)(2,1)S(1)} %bitcast.6, bf16[3,1281,1280]{2,1,0:T(8,128)(2,1)S(1)} %get-tuple-element.8.held_ref, bf16[5,1281,1280]{2,1,0:T(8,128)(2,1)} %leg_ref.3), custom_call_target="tpu_custom_call" | custom-call | tf_op jit(solution)/shard_map/transform/pallas_call | solution.py:300
Async XLA Ops:
  5.6 55.6 %copy-start = (s32[640]{0:T(1024)S(1)}, s32[640]{0:T(1024)}, u32[]{:S(2)}) copy-start(s32[640]{0:T(1024)} %pair_ref.1) | copy-start | bytes 7684

commit v4 on v3

--- a/solution.py
+++ b/solution.py
@@ -140,7 +140,7 @@
         out_ref[rows, :] = wide[rows, :].astype(jnp.bfloat16)
         return carry
 
-    lax.fori_loop(0, owners * CHUNK // block, pack, 0)
+    lax.fori_loop(0, owners * CHUNK // block, pack, 0, unroll=True)
     for copy in holds:
         copy.wait()
 

time: 68.7 us -> 68.6 us (level)
  no operation moved by 1% of the time
where the time goes in v4:
time: 68.6 us; the launch traced here: 68.5 us
  blocking collectives  55.6 us (81%)
  Pallas kernels  12.9 us (19%)
    all_to_all x1, blocking collectives, shards(): lax.all_to_all(chunks, ('lat', 'lev'), split_axis=0, concat_axis=0, tiled...  55.6 us
    pallas_call x1, Pallas kernels, transform(): pl.pallas_call(sum_kernel, out_shape=jax.ShapeDtypeStruct((slots, 64, cou...  7.42 us
    pallas_call x1, Pallas kernels, pick(): pl.pallas_call(pick_kernel, out_shape=(jax.ShapeDtypeStruct((owners * CHU...  5.48 us

profile of v4, /device:TPU:1, one launch (start us, length us, event | category | flops | bytes accessed | tf_op | source)
XLA Modules:
  0.0 68.5 jit_solution(6105960741283577455)
XLA Ops:
  0.0 5.5 %pick.1 = (bf16[13312,128]{1,0:T(8,128)(2,1)S(1)}, bf16[3,1281,1280]{2,1,0:T(8,128)(2,1)S(1)}) custom-call(s32[5,128]{1,0:T(8,128)} %bitcast.8, s32[10,128]{1,0:T(8,128)} %bitcast.10, bf16[8,160,1280]{2,1,0:T(8,128)(2,1)} %bitcast.9, bf16[5,1281,1280]{2,1,0:T(8,128)(2,1)} %leg_ref.3), custom_call_target="tpu_custom_call" | custom-call | tf_op jit(solution)/shard_map/pick/pallas_call | solution.py:266
  5.5 0.0 copy-start
  5.5 55.6 %all_to_all.5 = bf16[128,104,128]{2,1,0:T(8,128)(2,1)S(1)} all-to-all(bf16[128,104,128]{2,1,0:T(8,128)(2,1)S(1)} %bitcast.7), channel_id=1, replica_groups=mesh['lat'=16,'lev'=8] {'lat','lev'}, dimensions={0} | all-to-all | bytes 6815744 | tf_op jit(solution)/shard_map/all_to_all | solution.py:322
  61.1 0.0 copy-done
  61.1 7.4 %transform.1 = f32[5,64,1281]{2,1,0:T(8,128)} custom-call(s32[640]{0:T(1024)S(1)} %copy-done, bf16[13312,128]{1,0:T(8,128)(2,1)S(1)} %bitcast.6, bf16[3,1281,1280]{2,1,0:T(8,128)(2,1)S(1)} %get-tuple-element.8.held_ref, bf16[5,1281,1280]{2,1,0:T(8,128)(2,1)} %leg_ref.3), custom_call_target="tpu_custom_call" | custom-call | tf_op jit(solution)/shard_map/transform/pallas_call | solution.py:300
Async XLA Ops:
  5.5 55.6 %copy-start = (s32[640]{0:T(1024)S(1)}, s32[640]{0:T(1024)}, u32[]{:S(2)}) copy-start(s32[640]{0:T(1024)} %pair_ref.1) | copy-start | bytes 7684
